TPU v7x, 32 devices: a whole 2x2x4 slice. The times are simulated.
32 devices in a mesh: groups: 2 (over y), node: 4 (over z), tp: 4 (over x, core).
Axes of the slice: x: 2, y: 2, z: 4, core: 2. Of those that a mesh axis runs over, the one named last changes fastest.
Arguments:
- queries: bfloat16 [16, 256, 8192], P(('groups', 'node'), None, 'tp'), parts along dimension 0, may hold values from -72 to 72
- new_kv: bfloat16 [2, 16, 256, 1024], P(None, ('groups', 'node'), None, 'tp'), parts along dimension 1, may hold values from -6 to 6
- page_pool: bfloat16 [2, 256, 128, 1024], P(None, ('groups', 'node'), None, 'tp'), parts along dimension 1, may hold values from -6 to 6
- slot_request: int32 [16], P('groups'), parts along dimension 0, may hold values from 0 to 7, as said below
- prefix_len: int32 [16], P('groups'), parts along dimension 0, may hold values from 1 to 2048, as said below
- page_holder: int32 [16, 16], P('groups'), parts along dimension 0, may hold values from 0 to 3, as said below
- page_slot: int32 [16, 16], P('groups'), parts along dimension 0, may hold values from 0 to 31, as said below
- decode_slot: int32 [16], P('groups'), parts along dimension 0, may hold values from 0 to 7, as said below
Outputs:
- attended: bfloat16 [16, 256, 8192], P(('groups', 'node'), None, 'tp'), parts along dimension 0
- decode_kv: bfloat16 [2, 16, 256, 1024], P(None, ('groups', 'node'), None, 'tp'), parts along dimension 1
There are 2 independent parts, one for each index of `groups`. A program takes and returns all parts, laid end to end along the dimension named above; each array names one. Nothing has to cross between parts.
Inputs may be any that keep to these rules, and one draw needn't show every extreme that they name: `slot_request`: a permutation: each request stands in one prefill slot. `prefix_len`: the requests of some prefill node all have 16 * 128 prefix tokens. `page_holder`: entries j < ceil(prefix_len / 128) are used, the others arbitrary; one holder holds at most 8 used pages of the requests of one prefill node, and exactly 8 for some holder and node. `page_slot`: used pages of one holder lie in different slots; unused entries arbitrary. `decode_slot`: a permutation; slot s lies on decode node s // 2; two requests of one prefill node never share a decode node.
All inputs are finite; a program needn't handle non-finite values.
Results may differ from a plain program's by a relative error of at most 0.0032.
Values may be sent and summed in bfloat16 or wider, within the bound.
No kernel may reach another device: no remote copies, remote signals or barrier semaphores. Data moves between devices by JAX's collectives and lax.ppermute only.
A program may use at most 64 MiB of HBM per device.

v0:
```python
import functools
import math

import jax
import jax.numpy as jnp
from jax import lax
from jax.experimental import pallas as pl
from jax.experimental.pallas import tpu as pltpu
from jax.sharding import PartitionSpec as P

HD = 128
BLOCK_PAGES = 4
MASKED = -1e30
ANY = pl.BlockSpec(memory_space=pl.ANY)
VMEM = pl.BlockSpec(memory_space=pltpu.VMEM)


def message_plan(nodes, capacity):
    half = nodes // 2
    shifts = [half] * (nodes > 1) + [k for k in range(1, nodes) if k != half]
    cut = (capacity + 1) // 2
    stages = [[(k, 0, cut) for k in shifts]] if shifts else []
    if cut < capacity and shifts:
        stages.append([(k, cut, capacity) for k in shifts])
    return stages


def pages_of(prefix_len_ref, request, page_len):
    return lax.div(prefix_len_ref[request] + page_len - 1, page_len)


def pack_kernel(
    nodes, per_node, most_pages, page_len, messages,
    request_ref, len_ref, holder_ref, slot_ref, node_ref, pool_ref, new_ref, decode_ref,
    *rest,
):
    page_out = rest[: len(messages)]
    decode_out = rest[len(messages) : len(messages) + nodes - 1]
    source_ref, page_sem, decode_sem = rest[len(messages) + nodes - 1 :]
    me = node_ref[0]

    def page_copy(index, offset, slot):
        k, first, _ = messages[index]
        return pltpu.make_async_copy(
            pool_ref.at[:, slot], page_out[index].at[offset], page_sem.at[k - 1, first + offset]
        )

    counts = []
    for k in range(1, nodes):
        there = lax.rem(me + k, nodes)
        arrival = jnp.int32(0)
        for member in range(per_node):
            request = request_ref[there * per_node + member]
            page_total = pages_of(len_ref, request, page_len)

            def one_page(j, arrival, k=k, request=request):
                here = holder_ref[request, j] == me

                @pl.when(here)
                def _():
                    slot = slot_ref[request, j]
                    for index, (shift, first, last) in enumerate(messages):
                        if shift == k:

                            @pl.when((arrival >= first) & (arrival < last))
                            def _():
                                page_copy(index, arrival - first, slot).start()

                return arrival + here.astype(jnp.int32)

            arrival = lax.fori_loop(0, page_total, one_page, arrival)
        counts.append(arrival)

    def decode_copies(act):
        for k in range(1, nodes):
            there = lax.rem(me + k, nodes)
            for member in range(per_node):
                target = decode_ref[request_ref[me * per_node + member]]

                @pl.when(lax.div(target, per_node) == there)
                def _():
                    act(
                        pltpu.make_async_copy(
                            new_ref.at[:, member], decode_out[k - 1], decode_sem.at[k - 1]
                        )
                    )

    decode_copies(lambda copy: copy.start())

    def one_source(p, carry):
        wanted = decode_ref[request_ref[p]] - me * per_node

        @pl.when((wanted >= 0) & (wanted < per_node))
        def _():
            source_ref[2 * wanted] = lax.rem(me - lax.div(p, per_node) + nodes, nodes)
            source_ref[2 * wanted + 1] = lax.rem(p, per_node)

        return carry

    lax.fori_loop(0, nodes * per_node, one_source, 0)

    for index, (k, first, last) in enumerate(messages):
        for offset in range(last - first):

            @pl.when(first + offset < counts[k - 1])
            def _():
                page_copy(index, offset, 0).wait()

    decode_copies(lambda copy: copy.wait())


def head_pipeline(count, scores_of, place_of, top_ref, total_ref, acc_ref, score_ref, weight_ref, turned, rate, fresh, visible):
    def soften(h):
        place = place_of(h)
        scores = visible(score_ref[h % 2])
        top = jnp.max(scores, axis=0, keepdims=True)
        if not fresh:
            before = top_ref[place]
            top = jnp.maximum(before, top)
            fade = jnp.exp2((before - top) * rate)
            fade_of[h] = fade
        weights = jnp.exp2((scores - top) * rate)
        total = jnp.sum(weights, axis=0, keepdims=True)
        top_ref[place] = top
        total_ref[place] = total if fresh else total_ref[place] * fade + total
        weight_ref[h % 2] = weights.astype(weight_ref.dtype)

    def gather(h):
        place = place_of(h)
        product = jnp.dot(turned, weight_ref[h % 2], preferred_element_type=jnp.float32)
        acc_ref[place] = product if fresh else acc_ref[place] * fade_of[h] + product

    fade_of = {}
    for step in range(count + 2):
        if step < count:
            score_ref[step % 2] = scores_of(step)
        if 0 <= step - 2 < count:
            gather(step - 2)
        if 0 <= step - 1 < count:
            soften(step - 1)


def attend_kernel(
    nodes, per_node, most_pages, page_len, messages, opening, closing,
    request_ref, len_ref, holder_ref, slot_ref, node_ref, query_ref, *rest,
):
    if opening:
        new_ref, pool_ref = rest[:2]
        rest = rest[2:]
    else:
        old_acc, old_top, old_total = rest[:3]
        received = rest[3 : 3 + len(messages)]
        rest = rest[3 + len(messages) :]
    if closing:
        out_ref, acc_ref, top_ref, total_ref = rest[:4]
        rest = rest[4:]
    else:
        acc_ref, top_ref, total_ref = rest[:3]
        rest = rest[3:]
    page_ref, score_ref, weight_ref, arrival_ref, count_ref, page_sem = rest
    me = node_ref[0]
    width = page_ref.shape[-1]
    groups = width // HD
    per_group = query_ref.shape[2] // width
    heads = groups * per_group
    suffix = query_ref.shape[1]
    block_keys = BLOCK_PAGES * page_len
    rate = HD ** (-0.5) * math.log2(math.e)

    for holder in range(nodes):
        arrival_ref[holder] = 0
    for member in range(per_node):
        request = request_ref[me * per_node + member]

        def one_page(j, carry, request=request, member=member):
            count, keys = carry
            holder = holder_ref[request, j]
            arrival = arrival_ref[holder]
            arrival_ref[holder] = arrival + 1
            shift = lax.rem(me - holder + nodes, nodes)
            sem = page_sem.at[member, count]
            place = page_ref.at[member, count]
            if opening:
                taken = shift == 0

                @pl.when(taken)
                def _():
                    pltpu.make_async_copy(pool_ref.at[:, slot_ref[request, j]], place, sem).start()

            else:
                taken = jnp.bool_(False)
                for index, (k, first, last) in enumerate(messages):
                    match = (shift == k) & (arrival >= first) & (arrival < last)
                    taken = taken | match

                    @pl.when(match)
                    def _():
                        pltpu.make_async_copy(received[index].at[arrival - first], place, sem).start()

            filled = jnp.minimum(len_ref[request] - j * page_len, page_len)
            return (
                count + taken.astype(jnp.int32),
                keys + jnp.where(taken, filled, 0),
            )

        count, keys = lax.fori_loop(
            0, pages_of(len_ref, request, page_len), one_page, (jnp.int32(0), jnp.int32(0))
        )
        count_ref[0, member] = count
        count_ref[1, member] = keys

    def head_lanes(group, h):
        return pl.ds(pl.multiple_of((group * per_group + h) * HD, HD), HD)

    def over_groups(act):
        def one_group(i, carry):
            member, group = lax.div(i, groups), lax.rem(i, groups)
            act(member, group, pl.ds(pl.multiple_of(group * HD, HD), HD))
            return carry

        lax.fori_loop(0, per_node * groups, one_group, 0)

    if opening:
        row = lax.broadcasted_iota(jnp.int32, (suffix, suffix), 0)
        column = lax.broadcasted_iota(jnp.int32, (suffix, suffix), 1)

        def new_keys(member, group, lanes):
            keys_new = new_ref[0, member, :, lanes]
            values_new = new_ref[1, member, :, lanes].T

            def scores_of(h):
                query = query_ref[member, :, head_lanes(group, h)]
                return lax.dot_general(
                    keys_new, query, (((1,), (1,)), ((), ())), preferred_element_type=jnp.float32
                )

            head_pipeline(
                per_group, scores_of, lambda h: member * heads + group * per_group + h,
                top_ref, total_ref, acc_ref, score_ref.at[:, :suffix], weight_ref.at[:, :suffix], values_new, rate, True,
                lambda scores: jnp.where(row <= column, scores, MASKED),
            )

        over_groups(new_keys)
    else:
        acc_ref[...] = old_acc[...]
        top_ref[...] = old_top[...]
        total_ref[...] = old_total[...]

    def wait_member(member, carry):
        def wait_page(i, carry):
            pltpu.make_async_copy(page_ref.at[member, i], page_ref.at[member, i], page_sem.at[member, i]).wait()
            return carry

        return lax.fori_loop(0, count_ref[0, member], wait_page, carry)

    lax.fori_loop(0, per_node, wait_member, 0)

    def old_keys(member, group, lanes):
        def one_block(b, carry):
            pages = pl.ds(b * BLOCK_PAGES, BLOCK_PAGES)
            valid = count_ref[1, member] - b * block_keys

            block_key = page_ref[member, pages, 0, :, lanes].reshape(block_keys, HD)
            block_values = page_ref[member, pages, 1, :, lanes].reshape(block_keys, HD)
            row = lax.broadcasted_iota(jnp.int32, (block_keys, HD), 0)
            block_values = jnp.where(row < valid, block_values, jnp.zeros_like(block_values))

            def scores_of(h):
                query = query_ref[member, :, head_lanes(group, h)]
                return lax.dot_general(
                    block_key, query, (((1,), (1,)), ((), ())), preferred_element_type=jnp.float32
                )

            def visible(scores):
                row = lax.broadcasted_iota(jnp.int32, scores.shape, 0)
                return jnp.where(row < valid, scores, MASKED)

            head_pipeline(
                per_group, scores_of, lambda h: member * heads + group * per_group + h,
                top_ref, total_ref, acc_ref, score_ref, weight_ref, block_values.T, rate, False, visible,
            )
            return carry

        lax.fori_loop(0, lax.div(count_ref[0, member] + BLOCK_PAGES - 1, BLOCK_PAGES), one_block, 0)

    over_groups(old_keys)

    if closing:
        for member in range(per_node):

            def one_out(head, carry, member=member):
                place = member * heads + head
                result = acc_ref[place] * (1.0 / total_ref[place])
                out_ref[member, :, pl.ds(pl.multiple_of(head * HD, HD), HD)] = result.astype(out_ref.dtype).T
                return carry

            lax.fori_loop(0, heads, one_out, 0, unroll=2)


def attend(nodes, capacity, page_pool_dtype, page_shape, most_pages, tables, queries, stage, inputs, opening, closing):
    per_node, suffix, query_width = queries.shape
    page_len = page_shape[1]
    heads = query_width // HD
    state_shape = [
        jax.ShapeDtypeStruct((per_node * heads, HD, suffix), jnp.float32),
        jax.ShapeDtypeStruct((per_node * heads, 1, suffix), jnp.float32),
        jax.ShapeDtypeStruct((per_node * heads, 1, suffix), jnp.float32),
    ]

    slots = capacity if opening else sum(last - first for _, first, last in stage)
    slots = -(-min(slots, most_pages) // BLOCK_PAGES) * BLOCK_PAGES
    in_specs = [VMEM] + ([VMEM, ANY] if opening else [VMEM] * 3 + [ANY] * len(stage))
    out_specs = [VMEM] * (4 if closing else 3)
    result_shape = ([jax.ShapeDtypeStruct(queries.shape, queries.dtype)] if closing else []) + state_shape
    scratch = [
        pltpu.VMEM((per_node, slots) + page_shape, page_pool_dtype),
        pltpu.VMEM((2, BLOCK_PAGES * page_len, suffix), jnp.float32),
        pltpu.VMEM((2, BLOCK_PAGES * page_len, suffix), page_pool_dtype),
        pltpu.SMEM((nodes,), jnp.int32),
        pltpu.SMEM((2, per_node), jnp.int32),
        pltpu.SemaphoreType.DMA((per_node, slots)),
    ]
    if closing:
        out_specs = [VMEM]
        result_shape = result_shape[:1]
        scratch = [pltpu.VMEM(s.shape, s.dtype) for s in state_shape] + scratch
    work = (slots + (per_node * 2 if opening else 0)) * page_len * heads * suffix
    return pl.pallas_call(
        functools.partial(
            attend_kernel, nodes, per_node, most_pages, page_len, stage, opening, closing
        ),
        grid_spec=pltpu.PrefetchScalarGridSpec(
            num_scalar_prefetch=5, grid=(), in_specs=in_specs, out_specs=out_specs, scratch_shapes=scratch
        ),
        out_shape=result_shape,
        compiler_params=pltpu.CompilerParams(vmem_limit_bytes=40 * 1024 * 1024),
        cost_estimate=pl.CostEstimate(
            flops=work * 4 * HD * 2, bytes_accessed=12 * 1024 * 1024, transcendentals=work
        ),
        name="attend",
    )(*tables, queries, *inputs)


def body(queries, new_kv, page_pool, slot_request, prefix_len, page_holder, page_slot, decode_slot):
    nodes = lax.axis_size("node")
    me = lax.axis_index("node").astype(jnp.int32).reshape(1)
    per_node, suffix, query_width = queries.shape
    page_len, width = page_pool.shape[2:]
    most_pages = page_holder.shape[1]
    capacity = page_pool.shape[1] // nodes
    stages = message_plan(nodes, capacity)
    messages = [message for stage in stages for message in stage]
    tables = (slot_request, prefix_len, page_holder, page_slot, me)
    page_shape = (2, page_len, width)
    packed = pl.pallas_call(
        functools.partial(pack_kernel, nodes, per_node, most_pages, page_len, messages),
        grid_spec=pltpu.PrefetchScalarGridSpec(
            num_scalar_prefetch=5,
            grid=(),
            in_specs=[ANY, ANY, pl.BlockSpec(memory_space=pltpu.SMEM)],
            out_specs=[VMEM] * (len(messages) + nodes - 1) + [pl.BlockSpec(memory_space=pltpu.SMEM)],
            scratch_shapes=[
                pltpu.SemaphoreType.DMA((max(nodes - 1, 1), capacity)),
                pltpu.SemaphoreType.DMA((max(nodes - 1, 1),)),
            ],
        ),
        out_shape=[jax.ShapeDtypeStruct((last - first,) + page_shape, page_pool.dtype) for _, first, last in messages]
        + [jax.ShapeDtypeStruct((2, suffix, width), new_kv.dtype)] * (nodes - 1)
        + [jax.ShapeDtypeStruct((2 * per_node,), jnp.int32)],
        name="pack",
    )(*tables, page_pool, new_kv, decode_slot)

    waiting = dict(zip(messages, packed))
    handing, sources = packed[len(messages) : -1], packed[-1]
    attending = functools.partial(
        attend, nodes, capacity, page_pool.dtype, page_shape, most_pages, tables, queries
    )

    def shifted(array, k):
        return lax.ppermute(array, "node", [(i, (i + k) % nodes) for i in range(nodes)])

    def send_after(earlier, array, k):
        if earlier is not None:
            arrived[earlier], array = lax.optimization_barrier((arrived[earlier], array))
        return shifted(array, k)

    arrived, latest, handed = {}, {}, {}
    for stage in stages:
        for message in stage:
            k = message[0]
            arrived[message] = send_after(latest.get(k), waiting[message], k)
            latest[k] = message
    for k in latest:
        handed[k] = send_after(latest[k], handing[k - 1], k)

    state = attending([], [new_kv, page_pool], True, not stages)
    for index, stage in enumerate(stages):
        inputs = list(state) + [arrived[message] for message in stage]
        state = attending(stage, inputs, False, index == len(stages) - 1)
    slots = []
    for slot in range(per_node):
        shift, member = sources[2 * slot], sources[2 * slot + 1]
        chosen = new_kv[:, 0]
        for other in range(1, per_node):
            chosen = jnp.where(member == other, new_kv[:, other], chosen)
        for k in range(1, nodes):
            chosen = jnp.where(shift == k, handed[k], chosen)
        slots.append(chosen)
    return state[0], jnp.stack(slots, axis=1)


def solution(mesh):
    placed = (
        P(("groups", "node"), None, "tp"),
        P(None, ("groups", "node"), None, "tp"),
        P(None, ("groups", "node"), None, "tp"),
        P("groups"),
        P("groups"),
        P("groups", None),
        P("groups", None),
        P("groups"),
    )
    return jax.shard_map(
        body,
        mesh=mesh,
        in_specs=placed,
        out_specs=(P(("groups", "node"), None, "tp"), P(None, ("groups", "node"), None, "tp")),
        check_vma=False,
    )
```

profile of v0, /device:TPU:20, one launch (start us, length us, event | category | flops | bytes accessed | tf_op | source)
XLA Modules:
  0.0 132.3 jit_solution(1239663467498241377)
XLA Ops:
  0.7 5.8 %pack.1 = (bf16[4,2,128,256]{3,2,1,0:T(8,128)(2,1)}, bf16[4,2,128,256]{3,2,1,0:T(8,128)(2,1)}, bf16[4,2,128,256]{3,2,1,0:T(8,128)(2,1)}, bf16[4,2,128,256]{3,2,1...) custom-call(s32[8]{0:T(128)} %request_ref.7, ...), custom_call_target="tpu_custom_call" | custom-call | tf_op jit(solution)/shard_map/pack/pallas_call | solution.py:355
  6.5 0.8 collective-permute-start
  7.3 1.3 %collective-permute-start.1 = (bf16[4,2,128,256]{3,2,1,0:T(8,128)(2,1)}, bf16[4,2,128,256]{3,2,1,0:T(8,128)(2,1)S(1)}, u32[]{:S(2)}, u32[]{:S(2)}) collective-permute-start(bf16[4,2,128,256]{3,2,1,0:T(8,128)(2,1)} %get-tuple-element.36), channel_id=1, source_target_pairs={{0,4},{4,8},{8,12},{12,0},{1,5},{5,9},{9,13},{13,1},{2,6},{6,10},{... | collective-permute-start | bytes 1572872 | tf_op jit(solution)/shard_map/ppermute | solution.py:380
  8.6 1.1 collective-permute-start.2
  9.8 1.5 %fusion.10 = (s32[1]{0:T(128)}, s32[1]{0:T(128)}, s32[1]{0:T(128)}, s32[1]{0:T(128)}) fusion(s32[4]{0:T(128)} %get-tuple-element.54), kind=kLoop, calls=%fused_computation.13 | loop fusion | bytes 32 | tf_op jit(solution)/shard_map/slice | solution.py:402
  16.6 0.0 copy-start
  16.7 2.2 %copy-done = bf16[2,32,128,256]{3,2,1,0:T(8,128)(2,1)S(1)} copy-done((bf16[2,32,128,256]{3,2,1,0:T(8,128)(2,1)S(1)}, bf16[2,32,128,256]{3,2,1,0:T(8,128)(2,1)}, u32[]{:S(2)}) %copy-start) | copy-done | bytes 4194328
  18.8 15.0 %attend.3 = (f32[32,128,256]{2,1,0:T(8,128)S(1)}, f32[32,1,256]{2,1,0:T(1,128)S(1)}, f32[32,1,256]{2,1,0:T(1,128)S(1)}) custom-call(s32[8]{0:T(128)S(1)} %copy-done.4, s32[8]{0:T(128)S(1)} %copy-done.5, s32[8,16]{1,0:T(8,128)S(1)} %copy-done.2, s32[8,16]{1,0:T(8,128)S(1)} %copy-done.3, s32[1]{0:T(128)} %bitcast.node_ref, ...), custom_call_target="tpu_custom_call" | custom-call | flops 6442450944 | bytes 12582912 | tf_op jit(solution)/shard_map/attend/pallas_call | solution.py:328
  33.8 9.1 %collective-permute-done.rest_3_ = bf16[4,2,128,256]{3,2,1,0:T(8,128)(2,1)S(1)} collective-permute-done((bf16[4,2,128,256]{3,2,1,0:T(8,128)(2,1)}, bf16[4,2,128,256]{3,2,1,0:T(8,128)(2,1)S(1)}, u32[]{:S(2)}, u32[]{:S(2)}) %collective-permute-start) | collective-permute-done | bytes 524320 | tf_op jit(solution)/shard_map/ppermute | solution.py:380
  42.9 3.7 %collective-permute-start.3 = (bf16[4,2,128,256]{3,2,1,0:T(8,128)(2,1)S(1)}, bf16[4,2,128,256]{3,2,1,0:T(8,128)(2,1)S(1)}, u32[]{:S(2)}, u32[]{:S(2)}) collective-permute-start(bf16[4,2,128,256]{3,2,1,0:T(8,128)(2,1)S(1)} %copy-done.9), channel_id=1, source_target_pairs={{0,8},{4,12},{8,0},{12,4},{1,9},{5,13},{9,1},{13,5},{2,10},{6,14},... | collective-permute-start | bytes 1572872 | tf_op jit(solution)/shard_map/ppermute | solution.py:380
  46.6 19.8 %collective-permute-done.1.rest_4_ = bf16[4,2,128,256]{3,2,1,0:T(8,128)(2,1)S(1)} collective-permute-done((bf16[4,2,128,256]{3,2,1,0:T(8,128)(2,1)}, bf16[4,2,128,256]{3,2,1,0:T(8,128)(2,1)S(1)}, u32[]{:S(2)}, u32[]{:S(2)}) %collective-permute-start.1) | collective-permute-done | bytes 524320 | tf_op jit(solution)/shard_map/ppermute | solution.py:380
  66.4 9.5 %collective-permute-done.2.rest_5_ = bf16[4,2,128,256]{3,2,1,0:T(8,128)(2,1)S(1)} collective-permute-done((bf16[4,2,128,256]{3,2,1,0:T(8,128)(2,1)}, bf16[4,2,128,256]{3,2,1,0:T(8,128)(2,1)S(1)}, u32[]{:S(2)}, u32[]{:S(2)}) %collective-permute-start.2) | collective-permute-done | bytes 524320 | tf_op jit(solution)/shard_map/ppermute | solution.py:380
  75.9 2.4 %collective-permute-start.5 = (bf16[4,2,128,256]{3,2,1,0:T(8,128)(2,1)S(1)}, bf16[4,2,128,256]{3,2,1,0:T(8,128)(2,1)S(1)}, u32[]{:S(2)}, u32[]{:S(2)}) collective-permute-start(bf16[4,2,128,256]{3,2,1,0:T(8,128)(2,1)S(1)} %copy-done.7), channel_id=1, source_target_pairs={{0,12},{4,0},{8,4},{12,8},{1,13},{5,1},{9,5},{13,9},{2,14},{6,2},{... | collective-permute-start | bytes 1572872 | tf_op jit(solution)/shard_map/ppermute | solution.py:380
  78.3 16.5 %attend.4 = (f32[32,128,256]{2,1,0:T(8,128)S(1)}, f32[32,1,256]{2,1,0:T(1,128)S(1)}, f32[32,1,256]{2,1,0:T(1,128)S(1)}) custom-call(s32[8]{0:T(128)S(1)} %copy-done.4, s32[8]{0:T(128)S(1)} %copy-done.5, s32[8,16]{1,0:T(8,128)S(1)} %copy-done.2, s32[8,16]{1,0:T(8,128)S(1)} %copy-done.3, s32[1]{0:T(128)} %bitcast.node_ref, ...), custom_call_target="tpu_custom_call" | custom-call | flops 6442450944 | bytes 12582912 | tf_op jit(solution)/shard_map/attend/pallas_call | solution.py:328
  94.8 0.0 collective-permute-done.3.rest_3_
  94.9 0.1 collective-permute-start.7
  94.9 10.8 %collective-permute-done.4.rest_4_ = bf16[4,2,128,256]{3,2,1,0:T(8,128)(2,1)S(1)} collective-permute-done((bf16[4,2,128,256]{3,2,1,0:T(8,128)(2,1)S(1)}, bf16[4,2,128,256]{3,2,1,0:T(8,128)(2,1)S(1)}, u32[]{:S(2)}, u32[]{:S(2)}) %collective-permute-start.4) | collective-permute-done | bytes 524320 | tf_op jit(solution)/shard_map/ppermute | solution.py:380
  105.7 3.8 %collective-permute-done.5.rest_5_ = bf16[4,2,128,256]{3,2,1,0:T(8,128)(2,1)S(1)} collective-permute-done((bf16[4,2,128,256]{3,2,1,0:T(8,128)(2,1)S(1)}, bf16[4,2,128,256]{3,2,1,0:T(8,128)(2,1)S(1)}, u32[]{:S(2)}, u32[]{:S(2)}) %collective-permute-start.5) | collective-permute-done | bytes 524320 | tf_op jit(solution)/shard_map/ppermute | solution.py:380
  109.6 2.5 %collective-permute-start.6 = (bf16[2,256,256]{2,1,0:T(8,128)(2,1)S(1)}, bf16[2,256,256]{2,1,0:T(8,128)(2,1)S(1)}, u32[]{:S(2)}, u32[]{:S(2)}) collective-permute-start(bf16[2,256,256]{2,1,0:T(8,128)(2,1)S(1)} %copy-done.10), channel_id=1, source_target_pairs={{0,12},{4,0},{8,4},{12,8},{1,13},{5,1},{9,5},{13,9},{2,14},{6,2},{... | collective-permute-start | bytes 786440 | tf_op jit(solution)/shard_map/ppermute | solution.py:380
  112.0 19.2 %attend.5 = bf16[2,256,2048]{2,1,0:T(8,128)(2,1)} custom-call(s32[8]{0:T(128)S(1)} %copy-done.4, s32[8]{0:T(128)S(1)} %copy-done.5, s32[8,16]{1,0:T(8,128)S(1)} %copy-done.2, s32[8,16]{1,0:T(8,128)S(1)} %copy-done.3, s32[1]{0:T(128)} %bitcast.node_ref, bf16[2,256,2048]{2,1,0:T(8,128)(2,1)S(1)} %copy-done.6, f32[32,128,256]{2,1,0:T(8,128)S(1)} %get-tuple-element.42.rest_0_, ...), custom_call_target="tpu_custom_call" | custom-call | flops 6442450944 | bytes 12582912 | tf_op jit(solution)/shard_map/attend/pallas_call | solution.py:328
  131.3 0.0 collective-permute-done.7
  131.3 0.1 fusion.4
  131.4 0.1 pad_maximum_fusion
  131.5 0.8 copy.12
  (28 shorter events, 0.1 us)
Async XLA Ops:
  0.6 16.0 %copy-start.3 = (s32[8,16]{1,0:T(8,128)S(1)}, s32[8,16]{1,0:T(8,128)}, u32[]{:S(2)}) copy-start(s32[8,16]{1,0:T(8,128)} %slot_ref.7) | copy-start | bytes 1540
  0.6 16.0 %copy-start.2 = (s32[8,16]{1,0:T(8,128)S(1)}, s32[8,16]{1,0:T(8,128)}, u32[]{:S(2)}) copy-start(s32[8,16]{1,0:T(8,128)} %holder_ref.7) | copy-start | bytes 1540
  0.7 16.0 %copy-start.5 = (s32[8]{0:T(128)S(1)}, s32[8]{0:T(128)}, u32[]{:S(2)}) copy-start(s32[8]{0:T(128)} %len_ref.7) | copy-start | bytes 100
  0.7 16.0 %copy-start.4 = (s32[8]{0:T(128)S(1)}, s32[8]{0:T(128)}, u32[]{:S(2)}) copy-start(s32[8]{0:T(128)} %request_ref.7) | copy-start | bytes 100
  0.7 16.0 %copy-start.1 = (bf16[2,2,256,256]{3,2,1,0:T(8,128)(2,1)S(1)}, bf16[2,2,256,256]{3,2,1,0:T(8,128)(2,1)}, u32[]{:S(2)}) copy-start(bf16[2,2,256,256]{3,2,1,0:T(8,128)(2,1)} %new_ref.1) | copy-start | bytes 1572868
  0.7 16.0 %copy-start.6 = (bf16[2,256,2048]{2,1,0:T(8,128)(2,1)S(1)}, bf16[2,256,2048]{2,1,0:T(8,128)(2,1)}, u32[]{:S(2)}) copy-start(bf16[2,256,2048]{2,1,0:T(8,128)(2,1)} %query_ref.5) | copy-start | bytes 6291460
  6.5 36.4 %collective-permute-start = (bf16[4,2,128,256]{3,2,1,0:T(8,128)(2,1)}, bf16[4,2,128,256]{3,2,1,0:T(8,128)(2,1)S(1)}, u32[]{:S(2)}, u32[]{:S(2)}) collective-permute-start(bf16[4,2,128,256]{3,2,1,0:T(8,128)(2,1)} %get-tuple-element.33), channel_id=1, source_target_pairs={{0,8},{4,12},{8,0},{12,4},{1,9},{5,13},{9,1},{13,5},{2,10},{6,14},... | collective-permute-start | bytes 1572872 | tf_op jit(solution)/shard_map/ppermute | solution.py:380
  7.3 59.1 %collective-permute-start.1 = (bf16[4,2,128,256]{3,2,1,0:T(8,128)(2,1)}, bf16[4,2,128,256]{3,2,1,0:T(8,128)(2,1)S(1)}, u32[]{:S(2)}, u32[]{:S(2)}) collective-permute-start(bf16[4,2,128,256]{3,2,1,0:T(8,128)(2,1)} %get-tuple-element.36), channel_id=1, source_target_pairs={{0,4},{4,8},{8,12},{12,0},{1,5},{5,9},{9,13},{13,1},{2,6},{6,10},{... | collective-permute-start | bytes 1572872 | tf_op jit(solution)/shard_map/ppermute | solution.py:380
  8.6 67.3 %collective-permute-start.2 = (bf16[4,2,128,256]{3,2,1,0:T(8,128)(2,1)}, bf16[4,2,128,256]{3,2,1,0:T(8,128)(2,1)S(1)}, u32[]{:S(2)}, u32[]{:S(2)}) collective-permute-start(bf16[4,2,128,256]{3,2,1,0:T(8,128)(2,1)} %get-tuple-element.39), channel_id=1, source_target_pairs={{0,12},{4,0},{8,4},{12,8},{1,13},{5,1},{9,5},{13,9},{2,14},{6,2},{... | collective-permute-start | bytes 1572872 | tf_op jit(solution)/shard_map/ppermute | solution.py:380
  16.6 2.2 %copy-start = (bf16[2,32,128,256]{3,2,1,0:T(8,128)(2,1)S(1)}, bf16[2,32,128,256]{3,2,1,0:T(8,128)(2,1)}, u32[]{:S(2)}) copy-start(bf16[2,32,128,256]{3,2,1,0:T(8,128)(2,1)} %pool_ref.1) | copy-start | bytes 12582916
  18.8 24.0 %copy-start.9 = (bf16[4,2,128,256]{3,2,1,0:T(8,128)(2,1)S(1)}, bf16[4,2,128,256]{3,2,1,0:T(8,128)(2,1)}, u32[]{:S(2)}) copy-start(bf16[4,2,128,256]{3,2,1,0:T(8,128)(2,1)} %get-tuple-element.45) | copy-start | bytes 1572868
  18.8 47.5 %copy-start.8 = (bf16[4,2,128,256]{3,2,1,0:T(8,128)(2,1)S(1)}, bf16[4,2,128,256]{3,2,1,0:T(8,128)(2,1)}, u32[]{:S(2)}) copy-start(bf16[4,2,128,256]{3,2,1,0:T(8,128)(2,1)} %get-tuple-element.48) | copy-start | bytes 1572868
  18.8 57.1 %copy-start.7 = (bf16[4,2,128,256]{3,2,1,0:T(8,128)(2,1)S(1)}, bf16[4,2,128,256]{3,2,1,0:T(8,128)(2,1)}, u32[]{:S(2)}) copy-start(bf16[4,2,128,256]{3,2,1,0:T(8,128)(2,1)} %get-tuple-element.51) | copy-start | bytes 1572868
  42.9 52.0 %collective-permute-start.3 = (bf16[4,2,128,256]{3,2,1,0:T(8,128)(2,1)S(1)}, bf16[4,2,128,256]{3,2,1,0:T(8,128)(2,1)S(1)}, u32[]{:S(2)}, u32[]{:S(2)}) collective-permute-start(bf16[4,2,128,256]{3,2,1,0:T(8,128)(2,1)S(1)} %copy-done.9), channel_id=1, source_target_pairs={{0,8},{4,12},{8,0},{12,4},{1,9},{5,13},{9,1},{13,5},{2,10},{6,14},... | collective-permute-start | bytes 1572872 | tf_op jit(solution)/shard_map/ppermute | solution.py:380
  66.4 39.4 %collective-permute-start.4 = (bf16[4,2,128,256]{3,2,1,0:T(8,128)(2,1)S(1)}, bf16[4,2,128,256]{3,2,1,0:T(8,128)(2,1)S(1)}, u32[]{:S(2)}, u32[]{:S(2)}) collective-permute-start(bf16[4,2,128,256]{3,2,1,0:T(8,128)(2,1)S(1)} %copy-done.8), channel_id=1, source_target_pairs={{0,4},{4,8},{8,12},{12,0},{1,5},{5,9},{9,13},{13,1},{2,6},{6,10},{... | collective-permute-start | bytes 1572872 | tf_op jit(solution)/shard_map/ppermute | solution.py:380
  75.9 33.6 %collective-permute-start.5 = (bf16[4,2,128,256]{3,2,1,0:T(8,128)(2,1)S(1)}, bf16[4,2,128,256]{3,2,1,0:T(8,128)(2,1)S(1)}, u32[]{:S(2)}, u32[]{:S(2)}) collective-permute-start(bf16[4,2,128,256]{3,2,1,0:T(8,128)(2,1)S(1)} %copy-done.7), channel_id=1, source_target_pairs={{0,12},{4,0},{8,4},{12,8},{1,13},{5,1},{9,5},{13,9},{2,14},{6,2},{... | collective-permute-start | bytes 1572872 | tf_op jit(solution)/shard_map/ppermute | solution.py:380
  78.3 16.6 %copy-start.12 = (bf16[2,256,256]{2,1,0:T(8,128)(2,1)S(1)}, bf16[2,256,256]{2,1,0:T(8,128)(2,1)}, u32[]{:S(2)}) copy-start(bf16[2,256,256]{2,1,0:T(8,128)(2,1)} %get-tuple-element.56) | copy-start | bytes 786436
  78.3 27.5 %copy-start.11 = (bf16[2,256,256]{2,1,0:T(8,128)(2,1)S(1)}, bf16[2,256,256]{2,1,0:T(8,128)(2,1)}, u32[]{:S(2)}) copy-start(bf16[2,256,256]{2,1,0:T(8,128)(2,1)} %get-tuple-element.57) | copy-start | bytes 786436
  78.3 31.3 %copy-start.10 = (bf16[2,256,256]{2,1,0:T(8,128)(2,1)S(1)}, bf16[2,256,256]{2,1,0:T(8,128)(2,1)}, u32[]{:S(2)}) copy-start(bf16[2,256,256]{2,1,0:T(8,128)(2,1)} %get-tuple-element.55) | copy-start | bytes 786436
  94.9 36.4 %collective-permute-start.7 = (bf16[2,256,256]{2,1,0:T(8,128)(2,1)S(1)}, bf16[2,256,256]{2,1,0:T(8,128)(2,1)S(1)}, u32[]{:S(2)}, u32[]{:S(2)}) collective-permute-start(bf16[2,256,256]{2,1,0:T(8,128)(2,1)S(1)} %copy-done.12), channel_id=1, source_target_pairs={{0,8},{4,12},{8,0},{12,4},{1,9},{5,13},{9,1},{13,5},{2,10},{6,14},... | collective-permute-start | bytes 786440 | tf_op jit(solution)/shard_map/ppermute | solution.py:380
  105.7 25.5 %collective-permute-start.8 = (bf16[2,256,256]{2,1,0:T(8,128)(2,1)S(1)}, bf16[2,256,256]{2,1,0:T(8,128)(2,1)S(1)}, u32[]{:S(2)}, u32[]{:S(2)}) collective-permute-start(bf16[2,256,256]{2,1,0:T(8,128)(2,1)S(1)} %copy-done.11), channel_id=1, source_target_pairs={{0,4},{4,8},{8,12},{12,0},{1,5},{5,9},{9,13},{13,1},{2,6},{6,10},{... | collective-permute-start | bytes 786440 | tf_op jit(solution)/shard_map/ppermute | solution.py:380
  109.6 21.7 %collective-permute-start.6 = (bf16[2,256,256]{2,1,0:T(8,128)(2,1)S(1)}, bf16[2,256,256]{2,1,0:T(8,128)(2,1)S(1)}, u32[]{:S(2)}, u32[]{:S(2)}) collective-permute-start(bf16[2,256,256]{2,1,0:T(8,128)(2,1)S(1)} %copy-done.10), channel_id=1, source_target_pairs={{0,12},{4,0},{8,4},{12,8},{1,13},{5,1},{9,5},{13,9},{2,14},{6,2},{... | collective-permute-start | bytes 786440 | tf_op jit(solution)/shard_map/ppermute | solution.py:380
where the time goes:
time: 133 us; the launch traced here: 132 us
  Pallas kernels  56.5 us (42%)
  waiting for transfers between devices  53 us (40%)
  starting transfers between devices  11.9 us (9%)
  between operations  6.19 us (5%)
  local copies, waits for them, and re-layouts  4.54 us (3%)
    ppermute x9, waiting for transfers between devices, shifted(): lax.ppermute(array, 'node', [(i, (i + k) % nodes) for i in range(nodes)])  53 us
    pallas_call x3, Pallas kernels, attend(): pl.pallas_call(functools.partial(attend_kernel, nodes, per_node, most_pag...  50.7 us
    ppermute x9, starting transfers between devices, shifted(): lax.ppermute(array, 'node', [(i, (i + k) % nodes) for i in range(nodes)])  11.9 us
    pallas_call x1, Pallas kernels, body(): pl.pallas_call(functools.partial(pack_kernel, nodes, per_node, most_pages...  5.79 us
    unnamed x27, local copies, waits for them, and re-layouts  3.06 us
  transfers between devices with their start and end apart: 9, of which 5 were waited for; matrix products, arithmetic and copies ran while one was open for 1% of the time, Pallas kernels for 38%

commit v1 on v0

--- a/solution.py
+++ b/solution.py
@@ -9,7 +9,8 @@
 from jax.sharding import PartitionSpec as P
 
 HD = 128
-BLOCK_PAGES = 4
+OWN_BLOCK_PAGES = 4
+BLOCK_PAGES = 6
 MASKED = -1e30
 ANY = pl.BlockSpec(memory_space=pl.ANY)
 VMEM = pl.BlockSpec(memory_space=pltpu.VMEM)
@@ -164,7 +165,8 @@
     per_group = query_ref.shape[2] // width
     heads = groups * per_group
     suffix = query_ref.shape[1]
-    block_keys = BLOCK_PAGES * page_len
+    block_pages = score_ref.shape[1] // page_len
+    block_keys = block_pages * page_len
     rate = HD ** (-0.5) * math.log2(math.e)
 
     for holder in range(nodes):
@@ -257,7 +259,7 @@
 
     def old_keys(member, group, lanes):
         def one_block(b, carry):
-            pages = pl.ds(b * BLOCK_PAGES, BLOCK_PAGES)
+            pages = pl.ds(b * block_pages, block_pages)
             valid = count_ref[1, member] - b * block_keys
 
             block_key = page_ref[member, pages, 0, :, lanes].reshape(block_keys, HD)
@@ -281,7 +283,7 @@
             )
             return carry
 
-        lax.fori_loop(0, lax.div(count_ref[0, member] + BLOCK_PAGES - 1, BLOCK_PAGES), one_block, 0)
+        lax.fori_loop(0, lax.div(count_ref[0, member] + block_pages - 1, block_pages), one_block, 0)
 
     over_groups(old_keys)
 
@@ -308,14 +310,15 @@
     ]
 
     slots = capacity if opening else sum(last - first for _, first, last in stage)
-    slots = -(-min(slots, most_pages) // BLOCK_PAGES) * BLOCK_PAGES
+    block_pages = OWN_BLOCK_PAGES if opening else BLOCK_PAGES
+    slots = -(-min(slots, most_pages) // block_pages) * block_pages
     in_specs = [VMEM] + ([VMEM, ANY] if opening else [VMEM] * 3 + [ANY] * len(stage))
     out_specs = [VMEM] * (4 if closing else 3)
     result_shape = ([jax.ShapeDtypeStruct(queries.shape, queries.dtype)] if closing else []) + state_shape
     scratch = [
         pltpu.VMEM((per_node, slots) + page_shape, page_pool_dtype),
-        pltpu.VMEM((2, BLOCK_PAGES * page_len, suffix), jnp.float32),
-        pltpu.VMEM((2, BLOCK_PAGES * page_len, suffix), page_pool_dtype),
+        pltpu.VMEM((2, block_pages * page_len, suffix), jnp.float32),
+        pltpu.VMEM((2, block_pages * page_len, suffix), page_pool_dtype),
         pltpu.SMEM((nodes,), jnp.int32),
         pltpu.SMEM((2, per_node), jnp.int32),
         pltpu.SemaphoreType.DMA((per_node, slots)),

time: 133 us -> 131 us (0.985)
  the two profiles are of different devices: /device:TPU:20 before, /device:TPU:12 now
where the time goes in v1:
time: 131 us
  Pallas kernels  53.8 us (41%)
  waiting for transfers between devices  49.2 us (38%)
  starting transfers between devices  16.7 us (13%)
  between operations  6.21 us (5%)
  local copies, waits for them, and re-layouts  4.54 us (3%)
    ppermute x9, waiting for transfers between devices, shifted(): lax.ppermute(array, 'node', [(i, (i + k) % nodes) for i in range(nodes)])  49.2 us
    pallas_call x3, Pallas kernels, attend(): pl.pallas_call(functools.partial(attend_kernel, nodes, per_node, most_pag...  48.1 us
    ppermute x9, starting transfers between devices, shifted(): lax.ppermute(array, 'node', [(i, (i + k) % nodes) for i in range(nodes)])  16.7 us
    pallas_call x1, Pallas kernels, body(): pl.pallas_call(functools.partial(pack_kernel, nodes, per_node, most_pages...  5.72 us
    unnamed x27, local copies, waits for them, and re-layouts  3.06 us
  transfers between devices with their start and end apart: 9, of which 4 were waited for; matrix products, arithmetic and copies ran while one was open for 1% of the time, Pallas kernels for 37%

profile of v1, /device:TPU:12, one launch (start us, length us, event | category | flops | bytes accessed | tf_op | source)
XLA Modules:
  0.0 130.7 jit_solution(8790824420950485882)
XLA Ops:
  0.7 5.7 %pack.1 = (bf16[4,2,128,256]{3,2,1,0:T(8,128)(2,1)}, bf16[4,2,128,256]{3,2,1,0:T(8,128)(2,1)}, bf16[4,2,128,256]{3,2,1,0:T(8,128)(2,1)}, bf16[4,2,128,256]{3,2,1...) custom-call(s32[8]{0:T(128)} %request_ref.7, ...), custom_call_target="tpu_custom_call" | custom-call | tf_op jit(solution)/shard_map/pack/pallas_call | solution.py:358
  6.4 2.9 %collective-permute-start = (bf16[4,2,128,256]{3,2,1,0:T(8,128)(2,1)}, bf16[4,2,128,256]{3,2,1,0:T(8,128)(2,1)S(1)}, u32[]{:S(2)}, u32[]{:S(2)}) collective-permute-start(bf16[4,2,128,256]{3,2,1,0:T(8,128)(2,1)} %get-tuple-element.33), channel_id=1, source_target_pairs={{0,8},{4,12},{8,0},{12,4},{1,9},{5,13},{9,1},{13,5},{2,10},{6,14},... | collective-permute-start | bytes 1572872 | tf_op jit(solution)/shard_map/ppermute | solution.py:383
  9.4 2.0 %collective-permute-start.2 = (bf16[4,2,128,256]{3,2,1,0:T(8,128)(2,1)}, bf16[4,2,128,256]{3,2,1,0:T(8,128)(2,1)S(1)}, u32[]{:S(2)}, u32[]{:S(2)}) collective-permute-start(bf16[4,2,128,256]{3,2,1,0:T(8,128)(2,1)} %get-tuple-element.39), channel_id=1, source_target_pairs={{0,12},{4,0},{8,4},{12,8},{1,13},{5,1},{9,5},{13,9},{2,14},{6,2},{... | collective-permute-start | bytes 1572872 | tf_op jit(solution)/shard_map/ppermute | solution.py:383
  11.4 1.5 %fusion.10 = (s32[1]{0:T(128)}, s32[1]{0:T(128)}, s32[1]{0:T(128)}, s32[1]{0:T(128)}) fusion(s32[4]{0:T(128)} %get-tuple-element.54), kind=kLoop, calls=%fused_computation.13 | loop fusion | bytes 32 | tf_op jit(solution)/shard_map/slice | solution.py:405
  18.3 0.0 copy-start
  18.3 2.2 %copy-done = bf16[2,32,128,256]{3,2,1,0:T(8,128)(2,1)S(1)} copy-done((bf16[2,32,128,256]{3,2,1,0:T(8,128)(2,1)S(1)}, bf16[2,32,128,256]{3,2,1,0:T(8,128)(2,1)}, u32[]{:S(2)}) %copy-start) | copy-done | bytes 4194328
  20.5 14.9 %attend.3 = (f32[32,128,256]{2,1,0:T(8,128)S(1)}, f32[32,1,256]{2,1,0:T(1,128)S(1)}, f32[32,1,256]{2,1,0:T(1,128)S(1)}) custom-call(s32[8]{0:T(128)S(1)} %copy-done.4, s32[8]{0:T(128)S(1)} %copy-done.5, s32[8,16]{1,0:T(8,128)S(1)} %copy-done.2, s32[8,16]{1,0:T(8,128)S(1)} %copy-done.3, s32[1]{0:T(128)} %bitcast.node_ref, ...), custom_call_target="tpu_custom_call" | custom-call | flops 6442450944 | bytes 12582912 | tf_op jit(solution)/shard_map/attend/pallas_call | solution.py:331
  35.4 0.0 collective-permute-done.rest_3_
  35.5 1.0 collective-permute-start.3
  36.4 29.3 %collective-permute-done.1.rest_4_ = bf16[4,2,128,256]{3,2,1,0:T(8,128)(2,1)S(1)} collective-permute-done((bf16[4,2,128,256]{3,2,1,0:T(8,128)(2,1)}, bf16[4,2,128,256]{3,2,1,0:T(8,128)(2,1)S(1)}, u32[]{:S(2)}, u32[]{:S(2)}) %collective-permute-start.1) | collective-permute-done | bytes 524320 | tf_op jit(solution)/shard_map/ppermute | solution.py:383
  65.7 2.4 %collective-permute-start.4 = (bf16[4,2,128,256]{3,2,1,0:T(8,128)(2,1)S(1)}, bf16[4,2,128,256]{3,2,1,0:T(8,128)(2,1)S(1)}, u32[]{:S(2)}, u32[]{:S(2)}) collective-permute-start(bf16[4,2,128,256]{3,2,1,0:T(8,128)(2,1)S(1)} %copy-done.8), channel_id=1, source_target_pairs={{0,4},{4,8},{8,12},{12,0},{1,5},{5,9},{9,13},{13,1},{2,6},{6,10},{... | collective-permute-start | bytes 1572872 | tf_op jit(solution)/shard_map/ppermute | solution.py:383
  68.1 9.7 %collective-permute-done.2.rest_5_ = bf16[4,2,128,256]{3,2,1,0:T(8,128)(2,1)S(1)} collective-permute-done((bf16[4,2,128,256]{3,2,1,0:T(8,128)(2,1)}, bf16[4,2,128,256]{3,2,1,0:T(8,128)(2,1)S(1)}, u32[]{:S(2)}, u32[]{:S(2)}) %collective-permute-start.2) | collective-permute-done | bytes 524320 | tf_op jit(solution)/shard_map/ppermute | solution.py:383
  77.9 15.1 %attend.4 = (f32[32,128,256]{2,1,0:T(8,128)S(1)}, f32[32,1,256]{2,1,0:T(1,128)S(1)}, f32[32,1,256]{2,1,0:T(1,128)S(1)}) custom-call(s32[8]{0:T(128)S(1)} %copy-done.4, s32[8]{0:T(128)S(1)} %copy-done.5, s32[8,16]{1,0:T(8,128)S(1)} %copy-done.2, s32[8,16]{1,0:T(8,128)S(1)} %copy-done.3, s32[1]{0:T(128)} %bitcast.node_ref, ...), custom_call_target="tpu_custom_call" | custom-call | flops 6442450944 | bytes 12582912 | tf_op jit(solution)/shard_map/attend/pallas_call | solution.py:331
  93.0 0.0 collective-permute-done.3.rest_3_
  93.0 5.6 %collective-permute-start.7 = (bf16[2,256,256]{2,1,0:T(8,128)(2,1)S(1)}, bf16[2,256,256]{2,1,0:T(8,128)(2,1)S(1)}, u32[]{:S(2)}, u32[]{:S(2)}) collective-permute-start(bf16[2,256,256]{2,1,0:T(8,128)(2,1)S(1)} %copy-done.12), channel_id=1, source_target_pairs={{0,8},{4,12},{8,0},{12,4},{1,9},{5,13},{9,1},{13,5},{2,10},{6,14},... | collective-permute-start | bytes 786440 | tf_op jit(solution)/shard_map/ppermute | solution.py:383
  98.6 5.4 %collective-permute-done.4.rest_4_ = bf16[4,2,128,256]{3,2,1,0:T(8,128)(2,1)S(1)} collective-permute-done((bf16[4,2,128,256]{3,2,1,0:T(8,128)(2,1)S(1)}, bf16[4,2,128,256]{3,2,1,0:T(8,128)(2,1)S(1)}, u32[]{:S(2)}, u32[]{:S(2)}) %collective-permute-start.4) | collective-permute-done | bytes 524320 | tf_op jit(solution)/shard_map/ppermute | solution.py:383
  104.0 2.8 %collective-permute-start.8 = (bf16[2,256,256]{2,1,0:T(8,128)(2,1)S(1)}, bf16[2,256,256]{2,1,0:T(8,128)(2,1)S(1)}, u32[]{:S(2)}, u32[]{:S(2)}) collective-permute-start(bf16[2,256,256]{2,1,0:T(8,128)(2,1)S(1)} %copy-done.11), channel_id=1, source_target_pairs={{0,4},{4,8},{8,12},{12,0},{1,5},{5,9},{9,13},{13,1},{2,6},{6,10},{... | collective-permute-start | bytes 786440 | tf_op jit(solution)/shard_map/ppermute | solution.py:383
  106.8 4.8 %collective-permute-done.5.rest_5_ = bf16[4,2,128,256]{3,2,1,0:T(8,128)(2,1)S(1)} collective-permute-done((bf16[4,2,128,256]{3,2,1,0:T(8,128)(2,1)S(1)}, bf16[4,2,128,256]{3,2,1,0:T(8,128)(2,1)S(1)}, u32[]{:S(2)}, u32[]{:S(2)}) %collective-permute-start.5) | collective-permute-done | bytes 524320 | tf_op jit(solution)/shard_map/ppermute | solution.py:383
  111.6 18.0 %attend.5 = bf16[2,256,2048]{2,1,0:T(8,128)(2,1)} custom-call(s32[8]{0:T(128)S(1)} %copy-done.4, s32[8]{0:T(128)S(1)} %copy-done.5, s32[8,16]{1,0:T(8,128)S(1)} %copy-done.2, s32[8,16]{1,0:T(8,128)S(1)} %copy-done.3, s32[1]{0:T(128)} %bitcast.node_ref, bf16[2,256,2048]{2,1,0:T(8,128)(2,1)S(1)} %copy-done.6, f32[32,128,256]{2,1,0:T(8,128)S(1)} %get-tuple-element.42.rest_0_, ...), custom_call_target="tpu_custom_call" | custom-call | flops 6442450944 | bytes 12582912 | tf_op jit(solution)/shard_map/attend/pallas_call | solution.py:331
  129.6 0.0 collective-permute-done.7
  129.6 0.0 collective-permute-done.8
  129.7 0.1 fusion.4
  129.8 0.1 pad_maximum_fusion
  129.9 0.8 copy.12
  (28 shorter events, 0.1 us)
Async XLA Ops:
  0.6 17.6 %copy-start.3 = (s32[8,16]{1,0:T(8,128)S(1)}, s32[8,16]{1,0:T(8,128)}, u32[]{:S(2)}) copy-start(s32[8,16]{1,0:T(8,128)} %slot_ref.7) | copy-start | bytes 1540
  0.6 17.6 %copy-start.2 = (s32[8,16]{1,0:T(8,128)S(1)}, s32[8,16]{1,0:T(8,128)}, u32[]{:S(2)}) copy-start(s32[8,16]{1,0:T(8,128)} %holder_ref.7) | copy-start | bytes 1540
  0.7 17.6 %copy-start.5 = (s32[8]{0:T(128)S(1)}, s32[8]{0:T(128)}, u32[]{:S(2)}) copy-start(s32[8]{0:T(128)} %len_ref.7) | copy-start | bytes 100
  0.7 17.6 %copy-start.4 = (s32[8]{0:T(128)S(1)}, s32[8]{0:T(128)}, u32[]{:S(2)}) copy-start(s32[8]{0:T(128)} %request_ref.7) | copy-start | bytes 100
  0.7 17.6 %copy-start.1 = (bf16[2,2,256,256]{3,2,1,0:T(8,128)(2,1)S(1)}, bf16[2,2,256,256]{3,2,1,0:T(8,128)(2,1)}, u32[]{:S(2)}) copy-start(bf16[2,2,256,256]{3,2,1,0:T(8,128)(2,1)} %new_ref.1) | copy-start | bytes 1572868
  0.7 17.6 %copy-start.6 = (bf16[2,256,2048]{2,1,0:T(8,128)(2,1)S(1)}, bf16[2,256,2048]{2,1,0:T(8,128)(2,1)}, u32[]{:S(2)}) copy-start(bf16[2,256,2048]{2,1,0:T(8,128)(2,1)} %query_ref.5) | copy-start | bytes 6291460
  6.4 29.0 %collective-permute-start = (bf16[4,2,128,256]{3,2,1,0:T(8,128)(2,1)}, bf16[4,2,128,256]{3,2,1,0:T(8,128)(2,1)S(1)}, u32[]{:S(2)}, u32[]{:S(2)}) collective-permute-start(bf16[4,2,128,256]{3,2,1,0:T(8,128)(2,1)} %get-tuple-element.33), channel_id=1, source_target_pairs={{0,8},{4,12},{8,0},{12,4},{1,9},{5,13},{9,1},{13,5},{2,10},{6,14},... | collective-permute-start | bytes 1572872 | tf_op jit(solution)/shard_map/ppermute | solution.py:383
  9.4 56.3 %collective-permute-start.1 = (bf16[4,2,128,256]{3,2,1,0:T(8,128)(2,1)}, bf16[4,2,128,256]{3,2,1,0:T(8,128)(2,1)S(1)}, u32[]{:S(2)}, u32[]{:S(2)}) collective-permute-start(bf16[4,2,128,256]{3,2,1,0:T(8,128)(2,1)} %get-tuple-element.36), channel_id=1, source_target_pairs={{0,4},{4,8},{8,12},{12,0},{1,5},{5,9},{9,13},{13,1},{2,6},{6,10},{... | collective-permute-start | bytes 1572872 | tf_op jit(solution)/shard_map/ppermute | solution.py:383
  9.4 68.5 %collective-permute-start.2 = (bf16[4,2,128,256]{3,2,1,0:T(8,128)(2,1)}, bf16[4,2,128,256]{3,2,1,0:T(8,128)(2,1)S(1)}, u32[]{:S(2)}, u32[]{:S(2)}) collective-permute-start(bf16[4,2,128,256]{3,2,1,0:T(8,128)(2,1)} %get-tuple-element.39), channel_id=1, source_target_pairs={{0,12},{4,0},{8,4},{12,8},{1,13},{5,1},{9,5},{13,9},{2,14},{6,2},{... | collective-permute-start | bytes 1572872 | tf_op jit(solution)/shard_map/ppermute | solution.py:383
  18.3 2.2 %copy-start = (bf16[2,32,128,256]{3,2,1,0:T(8,128)(2,1)S(1)}, bf16[2,32,128,256]{3,2,1,0:T(8,128)(2,1)}, u32[]{:S(2)}) copy-start(bf16[2,32,128,256]{3,2,1,0:T(8,128)(2,1)} %pool_ref.1) | copy-start | bytes 12582916
  20.5 15.0 %copy-start.9 = (bf16[4,2,128,256]{3,2,1,0:T(8,128)(2,1)S(1)}, bf16[4,2,128,256]{3,2,1,0:T(8,128)(2,1)}, u32[]{:S(2)}) copy-start(bf16[4,2,128,256]{3,2,1,0:T(8,128)(2,1)} %get-tuple-element.45) | copy-start | bytes 1572868
  20.5 45.2 %copy-start.8 = (bf16[4,2,128,256]{3,2,1,0:T(8,128)(2,1)S(1)}, bf16[4,2,128,256]{3,2,1,0:T(8,128)(2,1)}, u32[]{:S(2)}) copy-start(bf16[4,2,128,256]{3,2,1,0:T(8,128)(2,1)} %get-tuple-element.48) | copy-start | bytes 1572868
  20.5 57.4 %copy-start.7 = (bf16[4,2,128,256]{3,2,1,0:T(8,128)(2,1)S(1)}, bf16[4,2,128,256]{3,2,1,0:T(8,128)(2,1)}, u32[]{:S(2)}) copy-start(bf16[4,2,128,256]{3,2,1,0:T(8,128)(2,1)} %get-tuple-element.51) | copy-start | bytes 1572868
  35.5 57.5 %collective-permute-start.3 = (bf16[4,2,128,256]{3,2,1,0:T(8,128)(2,1)S(1)}, bf16[4,2,128,256]{3,2,1,0:T(8,128)(2,1)S(1)}, u32[]{:S(2)}, u32[]{:S(2)}) collective-permute-start(bf16[4,2,128,256]{3,2,1,0:T(8,128)(2,1)S(1)} %copy-done.9), channel_id=1, source_target_pairs={{0,8},{4,12},{8,0},{12,4},{1,9},{5,13},{9,1},{13,5},{2,10},{6,14},... | collective-permute-start | bytes 1572872 | tf_op jit(solution)/shard_map/ppermute | solution.py:383
  65.7 38.2 %collective-permute-start.4 = (bf16[4,2,128,256]{3,2,1,0:T(8,128)(2,1)S(1)}, bf16[4,2,128,256]{3,2,1,0:T(8,128)(2,1)S(1)}, u32[]{:S(2)}, u32[]{:S(2)}) collective-permute-start(bf16[4,2,128,256]{3,2,1,0:T(8,128)(2,1)S(1)} %copy-done.8), channel_id=1, source_target_pairs={{0,4},{4,8},{8,12},{12,0},{1,5},{5,9},{9,13},{13,1},{2,6},{6,10},{... | collective-permute-start | bytes 1572872 | tf_op jit(solution)/shard_map/ppermute | solution.py:383
  77.8 33.7 %collective-permute-start.5 = (bf16[4,2,128,256]{3,2,1,0:T(8,128)(2,1)S(1)}, bf16[4,2,128,256]{3,2,1,0:T(8,128)(2,1)S(1)}, u32[]{:S(2)}, u32[]{:S(2)}) collective-permute-start(bf16[4,2,128,256]{3,2,1,0:T(8,128)(2,1)S(1)} %copy-done.7), channel_id=1, source_target_pairs={{0,12},{4,0},{8,4},{12,8},{1,13},{5,1},{9,5},{13,9},{2,14},{6,2},{... | collective-permute-start | bytes 1572872 | tf_op jit(solution)/shard_map/ppermute | solution.py:383
  77.8 15.1 %copy-start.12 = (bf16[2,256,256]{2,1,0:T(8,128)(2,1)S(1)}, bf16[2,256,256]{2,1,0:T(8,128)(2,1)}, u32[]{:S(2)}) copy-start(bf16[2,256,256]{2,1,0:T(8,128)(2,1)} %get-tuple-element.56) | copy-start | bytes 786436
  77.8 26.1 %copy-start.11 = (bf16[2,256,256]{2,1,0:T(8,128)(2,1)S(1)}, bf16[2,256,256]{2,1,0:T(8,128)(2,1)}, u32[]{:S(2)}) copy-start(bf16[2,256,256]{2,1,0:T(8,128)(2,1)} %get-tuple-element.57) | copy-start | bytes 786436
  77.9 33.7 %copy-start.10 = (bf16[2,256,256]{2,1,0:T(8,128)(2,1)S(1)}, bf16[2,256,256]{2,1,0:T(8,128)(2,1)}, u32[]{:S(2)}) copy-start(bf16[2,256,256]{2,1,0:T(8,128)(2,1)} %get-tuple-element.55) | copy-start | bytes 786436
  93.0 36.6 %collective-permute-start.7 = (bf16[2,256,256]{2,1,0:T(8,128)(2,1)S(1)}, bf16[2,256,256]{2,1,0:T(8,128)(2,1)S(1)}, u32[]{:S(2)}, u32[]{:S(2)}) collective-permute-start(bf16[2,256,256]{2,1,0:T(8,128)(2,1)S(1)} %copy-done.12), channel_id=1, source_target_pairs={{0,8},{4,12},{8,0},{12,4},{1,9},{5,13},{9,1},{13,5},{2,10},{6,14},... | collective-permute-start | bytes 786440 | tf_op jit(solution)/shard_map/ppermute | solution.py:383
  104.0 25.7 %collective-permute-start.8 = (bf16[2,256,256]{2,1,0:T(8,128)(2,1)S(1)}, bf16[2,256,256]{2,1,0:T(8,128)(2,1)S(1)}, u32[]{:S(2)}, u32[]{:S(2)}) collective-permute-start(bf16[2,256,256]{2,1,0:T(8,128)(2,1)S(1)} %copy-done.11), channel_id=1, source_target_pairs={{0,4},{4,8},{8,12},{12,0},{1,5},{5,9},{9,13},{13,1},{2,6},{6,10},{... | collective-permute-start | bytes 786440 | tf_op jit(solution)/shard_map/ppermute | solution.py:383
  111.6 18.1 %collective-permute-start.6 = (bf16[2,256,256]{2,1,0:T(8,128)(2,1)S(1)}, bf16[2,256,256]{2,1,0:T(8,128)(2,1)S(1)}, u32[]{:S(2)}, u32[]{:S(2)}) collective-permute-start(bf16[2,256,256]{2,1,0:T(8,128)(2,1)S(1)} %copy-done.10), channel_id=1, source_target_pairs={{0,12},{4,0},{8,4},{12,8},{1,13},{5,1},{9,5},{13,9},{2,14},{6,2},{... | collective-permute-start | bytes 786440 | tf_op jit(solution)/shard_map/ppermute | solution.py:383
